TPU v7x, 32 devices: a whole 2x2x4 slice. The times are simulated.
32 devices in a mesh: dp: 4 (over y, x), ctx: 8 (over z, core).
Axes of the slice: x: 2, y: 2, z: 4, core: 2. Of those that a mesh axis runs over, the one named last changes fastest.
Arguments:
- queries: bfloat16 [4, 1024, 1280], P('dp', 'ctx'), may hold values from -16 to 16
- keys: bfloat16 [4, 1024, 1280], P('dp', 'ctx'), may hold values from -16 to 16
- values: bfloat16 [4, 1024, 1280], P('dp', 'ctx'), may hold values from -6 to 6
- seg_lengths: int32 [4, 8], P('dp'), may hold values from 1 to 768, 1024 in all within a row
- out_grad: bfloat16 [4, 1024, 2560], P('dp', 'ctx'), may hold values from -6 to 6
- w_out: bfloat16 [1280, 2560], P('dp'), may hold values from -0.15625 to 0.15625
Outputs:
- attended: bfloat16 [4, 1024, 2560], P('dp', 'ctx')
- query_grad: bfloat16 [4, 1024, 1280], P('dp', 'ctx')
- key_grad: bfloat16 [4, 1024, 1280], P('dp', 'ctx')
- value_grad: bfloat16 [4, 1024, 1280], P('dp', 'ctx')
- w_out_grad: float32 [1280, 2560], P('dp')
Inputs may be any that keep to these rules, and one draw needn't show every extreme that they name: `seg_lengths`: each record's lengths sum to 1024; the longest of each record is exactly 768.
All inputs are finite; a program needn't handle non-finite values.
Results may differ from a plain program's by a relative error of at most 0.027.
Values may be sent and summed in bfloat16 or wider, within the bound.
A program may use at most 192 MiB of HBM per device.

v0:
```python
import math
import jax
import jax.numpy as jnp
from jax import lax
from jax.sharding import PartitionSpec as P

HEADS = 10
HD = 128
MASKED_SCORE = -1e30


def segment_ids(length_row, row_total):
    segment_ends = jnp.cumsum(length_row)
    positions = lax.iota(jnp.int32, row_total)
    return jnp.sum((segment_ends[None, :] <= positions[:, None]).astype(jnp.int32), axis=1)


def head_columns(matrix, head_index, head_width):
    return lax.dynamic_slice_in_dim(matrix, head_index * head_width, head_width, 1)


def take_rows(matrix, first_row, row_count):
    return lax.dynamic_slice_in_dim(matrix, first_row, row_count, 0)


def contract_last(left_side, right_side):
    return lax.dot_general(
        left_side, right_side, (((1,), (1,)), ((), ())), preferred_element_type=jnp.float32
    )


def contract_first(left_side, right_side):
    return lax.dot_general(
        left_side, right_side, (((0,), (0,)), ((), ())), preferred_element_type=jnp.float32
    )


def attend_forward(
    local_query, all_key, all_value, local_segments, all_segments, block_rows, score_scale
):
    local_rows = local_query.shape[0]
    all_rows = all_key.shape[0]
    block_count = all_rows // block_rows

    def one_head(head_index, carried):
        attention, log_norm, stored = carried
        query_head = head_columns(local_query, head_index, HD)
        key_head = head_columns(all_key, head_index, HD)
        value_head = head_columns(all_value, head_index, HD)
        head_scores = contract_last(query_head, key_head) * score_scale

        def block_scores(first_row):
            key_segments = take_rows(all_segments, first_row, block_rows)
            scores = lax.dynamic_slice_in_dim(head_scores, first_row, block_rows, 1)
            return (scores, local_segments[:, None] == key_segments[None, :])

        def stat_step(block_index, running):
            first_row = block_index * block_rows
            row_max, row_sum = running
            scores, same_segment = block_scores(first_row)
            new_max = jnp.maximum(
                row_max, jnp.max(jnp.where(same_segment, scores, MASKED_SCORE), axis=1)
            )
            shifted = jnp.where(same_segment, jnp.exp(scores - new_max[:, None]), 0.0)
            return (new_max, row_sum * jnp.exp(row_max - new_max) + jnp.sum(shifted, axis=1))

        start_state = (
            jnp.full((local_rows,), MASKED_SCORE, jnp.float32),
            jnp.zeros((local_rows,), jnp.float32),
        )
        row_max, row_sum = lax.fori_loop(0, block_count, stat_step, start_state)
        head_norm = row_max + jnp.log(row_sum)

        def value_step(block_index, accumulated):
            first_row = block_index * block_rows
            scores, same_segment = block_scores(first_row)
            soft_weights = jnp.where(
                same_segment, jnp.exp(scores - head_norm[:, None]), 0.0
            ).astype(jnp.bfloat16)
            value_block = take_rows(value_head, first_row, block_rows)
            return accumulated + jnp.dot(
                soft_weights, value_block, preferred_element_type=jnp.float32
            )

        summed = lax.fori_loop(0, block_count, value_step, jnp.zeros((local_rows, HD), jnp.float32))
        attention = lax.dynamic_update_slice_in_dim(
            attention, summed.astype(jnp.bfloat16), head_index * HD, 1
        )
        log_norm = lax.dynamic_update_slice_in_dim(log_norm, head_norm[:, None], head_index, 1)
        stored = lax.dynamic_update_slice_in_dim(stored, head_scores[None], head_index, 0)
        return (attention, log_norm, stored)

    start_triple = (
        jnp.zeros((local_rows, HEADS * HD), jnp.bfloat16),
        jnp.zeros((local_rows, HEADS), jnp.float32),
        jnp.zeros((HEADS, local_rows, all_rows), jnp.float32),
    )
    return lax.fori_loop(0, HEADS, one_head, start_triple)


def attend_backward(
    local_query,
    local_key,
    local_value,
    local_grad,
    local_norm,
    local_dot,
    all_query,
    all_key,
    all_value,
    all_grad,
    all_norm,
    all_dot,
    local_segments,
    all_segments,
    stored,
    block_rows,
    score_scale,
):
    local_rows = local_query.shape[0]
    block_count = all_key.shape[0] // block_rows

    def one_head(head_index, carried):
        query_grad, key_grad, value_grad = carried
        grad_head = head_columns(local_grad, head_index, HD)
        own_key = head_columns(local_key, head_index, HD)
        own_value = head_columns(local_value, head_index, HD)
        key_head = head_columns(all_key, head_index, HD)
        value_head = head_columns(all_value, head_index, HD)
        query_all = head_columns(all_query, head_index, HD)
        grad_all = head_columns(all_grad, head_index, HD)
        norm_head = head_columns(local_norm, head_index, 1)[:, 0]
        dot_head = head_columns(local_dot, head_index, 1)[:, 0]
        norm_all = head_columns(all_norm, head_index, 1)[:, 0]
        dot_all = head_columns(all_dot, head_index, 1)[:, 0]
        head_scores = lax.dynamic_index_in_dim(stored, head_index, 0, keepdims=False)

        def query_step(block_index, accumulated):
            first_row = block_index * block_rows
            key_segments = take_rows(all_segments, first_row, block_rows)
            key_block = take_rows(key_head, first_row, block_rows)
            value_block = take_rows(value_head, first_row, block_rows)
            scores = lax.dynamic_slice_in_dim(head_scores, first_row, block_rows, 1)
            same_segment = local_segments[:, None] == key_segments[None, :]
            probs = jnp.where(same_segment, jnp.exp(scores - norm_head[:, None]), 0.0)
            dprob = contract_last(grad_head, value_block)
            dscore = (probs * (dprob - dot_head[:, None])).astype(jnp.bfloat16)
            return accumulated + jnp.dot(dscore, key_block, preferred_element_type=jnp.float32)

        query_sum = lax.fori_loop(
            0, block_count, query_step, jnp.zeros((local_rows, HD), jnp.float32)
        )

        def key_step(block_index, running):
            first_row = block_index * block_rows
            query_segments = take_rows(all_segments, first_row, block_rows)
            key_sum, value_sum = running
            query_block = take_rows(query_all, first_row, block_rows)
            grad_block = take_rows(grad_all, first_row, block_rows)
            norm_block = take_rows(norm_all, first_row, block_rows)
            dot_block = take_rows(dot_all, first_row, block_rows)
            scores = contract_last(query_block, own_key) * score_scale
            same_segment = query_segments[:, None] == local_segments[None, :]
            probs = jnp.where(same_segment, jnp.exp(scores - norm_block[:, None]), 0.0)
            dprob = contract_last(grad_block, own_value)
            dscore = (probs * (dprob - dot_block[:, None])).astype(jnp.bfloat16)
            key_sum = key_sum + contract_first(dscore, query_block)
            value_sum = value_sum + contract_first(probs.astype(jnp.bfloat16), grad_block)
            return (key_sum, value_sum)

        zeros = jnp.zeros((local_rows, HD), jnp.float32)
        key_sum, value_sum = lax.fori_loop(0, block_count, key_step, (zeros, zeros))
        query_grad = lax.dynamic_update_slice_in_dim(
            query_grad, (query_sum * score_scale).astype(jnp.bfloat16), head_index * HD, 1
        )
        key_grad = lax.dynamic_update_slice_in_dim(
            key_grad, (key_sum * score_scale).astype(jnp.bfloat16), head_index * HD, 1
        )
        value_grad = lax.dynamic_update_slice_in_dim(
            value_grad, value_sum.astype(jnp.bfloat16), head_index * HD, 1
        )
        return (query_grad, key_grad, value_grad)

    empty = jnp.zeros((local_rows, HEADS * HD), jnp.bfloat16)
    return lax.fori_loop(0, HEADS, one_head, (empty, empty, empty))


def local(queries, keys, values, seg_lengths, out_grad, w_out):
    score_scale = 1.0 / math.sqrt(HD)
    local_rows = queries.shape[1]
    all_rows = local_rows * lax.axis_size("ctx")
    block_rows = min(all_rows, 512)
    local_query = queries[0]
    local_key = keys[0]
    local_value = values[0]
    local_outgrad = out_grad[0]
    all_segments = segment_ids(seg_lengths[0], all_rows)
    local_segments = take_rows(all_segments, lax.axis_index("ctx") * local_rows, local_rows)
    full_weight = lax.all_gather(w_out, "dp", axis=0, tiled=True)
    attn_grad = contract_last(local_outgrad, full_weight).astype(jnp.bfloat16)
    all_key, all_value, all_query, all_grad = (
        lax.all_gather(local_key, "ctx", axis=0, tiled=True),
        lax.all_gather(local_value, "ctx", axis=0, tiled=True),
        lax.all_gather(local_query, "ctx", axis=0, tiled=True),
        lax.all_gather(attn_grad, "ctx", axis=0, tiled=True),
    )
    attention, log_norm, stored = attend_forward(
        local_query, all_key, all_value, local_segments, all_segments, block_rows, score_scale
    )
    attended = jnp.dot(attention, full_weight, preferred_element_type=jnp.float32).astype(
        jnp.bfloat16
    )
    products = attn_grad.astype(jnp.float32) * attention.astype(jnp.float32)
    grad_dot = jnp.sum(products.reshape(local_rows, HEADS, HD), axis=2)
    all_norm, all_dot = (
        lax.all_gather(log_norm, "ctx", axis=0, tiled=True),
        lax.all_gather(grad_dot, "ctx", axis=0, tiled=True),
    )
    query_grad, key_grad, value_grad = attend_backward(
        local_query,
        local_key,
        local_value,
        attn_grad,
        log_norm,
        grad_dot,
        all_query,
        all_key,
        all_value,
        all_grad,
        all_norm,
        all_dot,
        local_segments,
        all_segments,
        stored,
        block_rows,
        score_scale,
    )
    grad_share = lax.psum_scatter(
        contract_first(attention, local_outgrad).astype(jnp.bfloat16),
        "dp",
        scatter_dimension=0,
        tiled=True,
    )
    weight_grad = lax.psum(grad_share, "ctx").astype(jnp.float32)
    return (attended[None], query_grad[None], key_grad[None], value_grad[None], weight_grad)


def solution(mesh):
    in_specs = (
        P("dp", "ctx", None),
        P("dp", "ctx", None),
        P("dp", "ctx", None),
        P("dp", None),
        P("dp", "ctx", None),
        P("dp", None),
    )
    out_specs = (
        P("dp", "ctx", None),
        P("dp", "ctx", None),
        P("dp", "ctx", None),
        P("dp", "ctx", None),
        P("dp", None),
    )
    return jax.shard_map(local, mesh=mesh, in_specs=in_specs, out_specs=out_specs, check_vma=False)
```

profile of v0, /device:TPU:0, one launch (start us, length us, event | category | flops | bytes accessed | tf_op | source)
XLA Modules:
  0.0 421.3 jit_solution(8447683285333391024)
XLA Ops:
  10.5 35.8 %all-gather.13.cloned.1.call-done = bf16[1,1024,1280]{2,1,0:T(8,128)(2,1)} async-done(((bf16[1,128,1280]{2,1,0:T(8,128)(2,1)}), bf16[1,1024,1280]{2,1,0:T(8,128)(2,1)}) %all-gather.13.cloned.1.call-update) | async-done | bytes 2621456 | tf_op jit(solution)/shard_map/all_gather | solution.py:202
  46.3 34.5 %all-gather.15.cloned.1.call-done = bf16[1,1024,1280]{2,1,0:T(8,128)(2,1)} async-done(((bf16[1,128,1280]{2,1,0:T(8,128)(2,1)}), bf16[1,1024,1280]{2,1,0:T(8,128)(2,1)}) %all-gather.15.cloned.1.call-update) | async-done | bytes 2621456 | tf_op jit(solution)/shard_map/all_gather | solution.py:203
  80.8 48.7 %while.152 = (s32[]{:T(128)}, bf16[128,1280]{1,0:T(8,128)(2,1)S(1)}, f32[128,10]{0,1:T(8,128)S(1)}, f32[10,128,1024]{2,1,0:T(8,128)}, bf16[128,1280]{1,0:T(8,128...) while((s32[]{:T(128)}, bf16[128,1280]{1,0:T(8,128)(2,1)S(1)}, ...), condition=%wide.region_9.10_spmd, body=%wide.region_2.9_spmd.sunk | while | flops 51233556 | bytes 3044121 | solution.py:98
  80.9 2.0 bitcast_dynamic-update-slice_fusion.2
  85.7 2.0 bitcast_dynamic-update-slice_fusion.2
  90.7 2.0 bitcast_dynamic-update-slice_fusion.2
  100.4 2.0 bitcast_dynamic-update-slice_fusion.2
  105.3 2.0 bitcast_dynamic-update-slice_fusion.2
  110.1 2.0 bitcast_dynamic-update-slice_fusion.2
  115.0 2.0 bitcast_dynamic-update-slice_fusion.2
  124.7 2.0 bitcast_dynamic-update-slice_fusion.2
  129.6 4.6 %convolution_convert_fusion = bf16[1280,2560]{1,0:T(8,128)(2,1)} fusion(bf16[128,1280]{1,0:T(8,128)(2,1)S(1)} %get-tuple-element.1124, bf16[1,128,2560]{2,1,0:T(8,128)(2,1)S(1)} %copy-done), kind=kOutput, calls=%fused_computation.82 | convolution fusion | flops 842137600 | bytes 7536640 | tf_op jit(solution)/shard_map/dot_general | solution.py:33
  134.9 19.2 %all-gather.9.cloned.1.call-done = bf16[1280,2560]{1,0:T(8,128)(2,1)} async-done(((bf16[320,2560]{1,0:T(8,128)(2,1)}), bf16[1280,2560]{1,0:T(8,128)(2,1)}) %all-gather.9.cloned.1.call-update) | async-done | bytes 6553616 | tf_op jit(solution)/shard_map/all_gather | solution.py:199
  154.1 5.8 %convert_multiply_fusion = (f32[128,1280]{1,0:T(8,128)S(1)}, bf16[128,1280]{1,0:T(8,128)(2,1)}) fusion(bf16[128,1280]{1,0:T(8,128)(2,1)S(1)} %get-tuple-element.1124, bf16[1280,2560]{1,0:T(8,128)(2,1)} %all-gather.9.cloned.1.call-done, bf16[1,128,2560]{2,1,0:T(8,128)(2,1)S(1)} %copy-done), kind=kOutput, calls=%fused_computation.88 | convolution fusion | flops 839516160 | bytes 8519680 | tf_op jit(solution)/shard_map/dot_general | solution.py:27
  159.9 14.0 %all_gather.26 = f32[1024,10]{0,1:T(8,128)S(1)} all-gather(f32[128,10]{0,1:T(8,128)S(1)} %get-tuple-element.2072), channel_id=1, replica_groups=mesh['dp'=4,'ctx'=8] {'ctx'}, dimensions={0}, use_global_device_ids=true | all-gather | bytes 46080 | tf_op jit(solution)/shard_map/all_gather | solution.py:216
  174.2 13.9 %all_gather.27 = f32[1024,10]{0,1:T(8,128)S(1)} all-gather(f32[128,10]{0,1:T(8,128)S(1)} %reduce_sum.32), channel_id=1, replica_groups=mesh['dp'=4,'ctx'=8] {'ctx'}, dimensions={0}, use_global_device_ids=true | all-gather | bytes 46080 | tf_op jit(solution)/shard_map/all_gather | solution.py:217
  188.2 4.9 %fusion.56 = bf16[1,128,2560]{2,1,0:T(8,128)(2,1)} fusion(bf16[128,1280]{1,0:T(8,128)(2,1)S(1)} %get-tuple-element.1124, bf16[1280,2560]{1,0:T(8,128)(2,1)} %all-gather.9.cloned.1.call-done), kind=kOutput, calls=%fused_computation.84 | convolution fusion | flops 839188480 | bytes 7536640 | tf_op jit(solution)/shard_map/dot_general | solution.py:210
  193.0 36.4 %reduce-scatter.2.cloned.1.call-done = bf16[320,2560]{1,0:T(8,128)(2,1)} async-done(((bf16[1280,2560]{1,0:T(8,128)(2,1)}), bf16[320,2560]{1,0:T(8,128)(2,1)}) %reduce-scatter.2.cloned.1.call-update) | async-done | bytes 1638416 | tf_op jit(solution)/shard_map/reduce_scatter | solution.py:238
  229.4 35.4 %all-gather.17.cloned.1.call-done = bf16[1,1024,1280]{2,1,0:T(8,128)(2,1)} async-done(((bf16[1,128,1280]{2,1,0:T(8,128)(2,1)}), bf16[1,1024,1280]{2,1,0:T(8,128)(2,1)}) %all-gather.17.cloned.1.call-update) | async-done | bytes 2621456 | tf_op jit(solution)/shard_map/all_gather | solution.py:204
  264.8 35.0 %all-gather.11.cloned.1.call-done = bf16[1024,1280]{1,0:T(8,128)(2,1)} async-done(((bf16[128,1280]{1,0:T(8,128)(2,1)}), bf16[1024,1280]{1,0:T(8,128)(2,1)}) %all-gather.11.cloned.1.call-update) | async-done | bytes 2621456 | tf_op jit(solution)/shard_map/all_gather | solution.py:205
  299.9 110.6 %while.155 = (s32[]{:T(128)}, bf16[128,1280]{1,0:T(8,128)(2,1)S(1)}, bf16[128,1280]{1,0:T(8,128)(2,1)S(1)}, bf16[128,1280]{1,0:T(8,128)(2,1)S(1)}, bf16[1024,128...) while((s32[]{:T(128)}, bf16[128,1280]{1,0:T(8,128)(2,1)S(1)}, ...), condition=%wide.region_16.17_spmd, body=%wide.region_11.16_spmd.sunk | while | flops 101761040 | bytes 7062036 | solution.py:185
  308.5 2.3 while.159
  319.6 2.3 while.159
  330.7 2.3 while.159
  341.7 2.3 while.159
  352.8 2.3 while.159
  363.9 2.3 while.159
  374.9 2.3 while.159
  386.0 2.3 while.159
  397.0 2.3 while.159
  408.1 2.3 while.159
  410.6 3.8 convert_element_type.83
  (636 shorter events, 171.0 us)
Async XLA Ops:
  7.2 122.4 %copy-start = (bf16[1,128,2560]{2,1,0:T(8,128)(2,1)S(1)}, bf16[1,128,2560]{2,1,0:T(8,128)(2,1)}, u32[]{:S(2)}) copy-start(bf16[1,128,2560]{2,1,0:T(8,128)(2,1)} %param.22) | copy-start | bytes 1966084
  7.2 39.1 %all-gather.13.cloned.1.call-start = ((), (), s32[]{:S(2)}) async-start(), calls=%async_computation.5 | async-start | bytes 2949120 | tf_op jit(solution)/shard_map/all_gather | solution.py:202
  7.9 72.9 %all-gather.15.cloned.1.call-start = ((), (), s32[]{:S(2)}) async-start(), calls=%async_computation.6 | async-start | bytes 2949120 | tf_op jit(solution)/shard_map/all_gather | solution.py:203
  8.7 145.4 %all-gather.9.cloned.1.call-start = ((), (), s32[]{:S(2)}) async-start(), calls=%async_computation.1 | async-start | bytes 8192000 | tf_op jit(solution)/shard_map/all_gather | solution.py:199
  9.4 220.0 %reduce-scatter.2.cloned.1.call-start = ((), (), s32[]{:S(2)}) async-start(), calls=%async_computation.3 | async-start | bytes 8192000 | tf_op jit(solution)/shard_map/reduce_scatter | solution.py:238
  134.2 130.6 %all-gather.17.cloned.1.call-start = ((), (), s32[]{:S(2)}) async-start(), calls=%async_computation.7 | async-start | bytes 2949120 | tf_op jit(solution)/shard_map/all_gather | solution.py:204
  134.8 165.0 %all-gather.11.cloned.1.call-start = ((), (), s32[]{:S(2)}) async-start(), calls=%async_computation.2 | async-start | bytes 2949120 | tf_op jit(solution)/shard_map/all_gather | solution.py:205
  159.9 250.7 %all-reduce.2.cloned.1.call-start = ((), (), s32[]{:S(2)}) async-start(), calls=%async_computation.4 | async-start | bytes 3276800 | tf_op jit(solution)/shard_map/psum | solution.py:244
  410.5 3.9 copy-start.1
  410.5 3.9 copy-start.2
  410.5 3.9 copy-start.3
Sparse Core Ops, SparseCore 0:
  9.7 36.5 all-gather.12
  47.9 32.8 all-gather.14
  82.7 71.3 all-gather.8
  157.0 72.3 reduce-scatter.1
  230.9 33.8 all-gather.16
  266.9 32.8 all-gather.10
  302.2 61.1 all-reduce.1
where the time goes:
time: 426 us; the launch traced here: 421 us
  waiting for transfers between devices  199 us (47%)
  local copies, waits for them, and re-layouts  94.9 us (22%)
  matrix products  66.7 us (16%)
  blocking collectives  28 us (7%)
  between operations  14.3 us (3%)
  other arithmetic  13.7 us (3%)
  loops' own time  4.48 us (1%)
    dynamic_slice x120, local copies, waits for them, and re-layouts, head_columns(): lax.dynamic_slice_in_dim(matrix, head_index * head_width, head_width, 1)  72.1 us
    reduce_scatter x1, waiting for transfers between devices, local(): lax.psum_scatter(contract_first(attention, local_outgrad).astype(jnp.bflo...  36.4 us
    all_gather x1, waiting for transfers between devices, local(): lax.all_gather(local_key, 'ctx', axis=0, tiled=True)  35.8 us
    all_gather x1, waiting for transfers between devices, local(): lax.all_gather(local_query, 'ctx', axis=0, tiled=True)  35.4 us
    all_gather x1, waiting for transfers between devices, local(): lax.all_gather(attn_grad, 'ctx', axis=0, tiled=True)  35 us
    all_gather x1, waiting for transfers between devices, local(): lax.all_gather(local_value, 'ctx', axis=0, tiled=True)  34.5 us
    dot_general x31, matrix products, contract_last(): lax.dot_general(left_side, right_side, (((1,), (1,)), ((), ())), preferre...  30.4 us
    all_gather x1, waiting for transfers between devices, local(): full_weight = lax.all_gather(w_out, 'dp', axis=0, tiled=True)  19.2 us
  transfers between devices with their start and end apart: 7, of which 6 were waited for; matrix products, arithmetic and copies ran while one was open for 41% of the time, Pallas kernels for 0%

commit v1 on v0

--- a/solution.py
+++ b/solution.py
@@ -196,7 +196,12 @@
     local_outgrad = out_grad[0]
     all_segments = segment_ids(seg_lengths[0], all_rows)
     local_segments = take_rows(all_segments, lax.axis_index("ctx") * local_rows, local_rows)
-    full_weight = lax.all_gather(w_out, "dp", axis=0, tiled=True)
+    ring = [w_out]
+    for hop in range(3):
+        ring.append(lax.ppermute(ring[-1], "dp", [(dev, (dev + 1) % 4) for dev in range(4)]))
+    full_weight = jnp.roll(
+        jnp.concatenate(ring[::-1], axis=0), (lax.axis_index("dp") + 1) * ring[0].shape[0], axis=0
+    )
     attn_grad = contract_last(local_outgrad, full_weight).astype(jnp.bfloat16)
     all_key, all_value, all_query, all_grad = (
         lax.all_gather(local_key, "ctx", axis=0, tiled=True),

time: 426 us -> 473 us (1.11)
  waiting for transfers between devices: 199 us -> 233 us
  local copies, waits for them, and re-layouts: 94.9 us -> 107 us
    ppermute x0 -> x3, waiting for transfers between devices: none -> 159 us  [local(): lax.ppermute(ring[-1], 'dp', [(dev, (dev + 1) % 4) for dev in range(4)])]
    reduce_scatter x1, waiting for transfers between devices: 36.4 us -> 0.01 us  [local(): lax.psum_scatter(contract_first(attention, local_outgrad).astype(jnp.bflo...]
    all_gather x1, waiting for transfers between devices: 35.4 us -> 0.02 us  [local(): lax.all_gather(local_query, 'ctx', axis=0, tiled=True)]
    all_gather x1, waiting for transfers between devices: 35 us -> 1.74 us  [local(): lax.all_gather(attn_grad, 'ctx', axis=0, tiled=True)]
    all_gather x1 -> x0, waiting for transfers between devices: 19.2 us -> none  [local(): full_weight = lax.all_gather(w_out, 'dp', axis=0, tiled=True)]
    dynamic_slice x20 -> x0, local copies, waits for them, and re-layouts: 12.8 us -> none  [one_head(): lax.dynamic_index_in_dim(stored, head_index, 0, keepdims=False)]
    unnamed x8 -> x23, local copies, waits for them, and re-layouts: 0.03 us -> 12.4 us
    squeeze x0 -> x10, local copies, waits for them, and re-layouts: none -> 10.9 us  [one_head(): lax.dynamic_index_in_dim(stored, head_index, 0, keepdims=False)]
  transfers between devices with their start and end apart: 7 -> 9, of which waited for: 6 -> 6; matrix products, arithmetic and copies ran while one was open for 41% -> 26% of each run, Pallas kernels for 0% -> 0%
where the time goes in v1:
time: 473 us; the launch traced here: 468 us
  waiting for transfers between devices  233 us (49%)
  local copies, waits for them, and re-layouts  107 us (23%)
  matrix products  63.4 us (13%)
  blocking collectives  28.2 us (6%)
  between operations  14.4 us (3%)
  other arithmetic  13.7 us (3%)
  loops' own time  4.77 us (1%)
    ppermute x3, waiting for transfers between devices, local(): lax.ppermute(ring[-1], 'dp', [(dev, (dev + 1) % 4) for dev in range(4)])  159 us
    dynamic_slice x130, local copies, waits for them, and re-layouts, head_columns(): lax.dynamic_slice_in_dim(matrix, head_index * head_width, head_width, 1)  73.3 us
    all_gather x1, waiting for transfers between devices, local(): lax.all_gather(local_key, 'ctx', axis=0, tiled=True)  36.5 us
    all_gather x1, waiting for transfers between devices, local(): lax.all_gather(local_value, 'ctx', axis=0, tiled=True)  34.5 us
    dot_general x31, matrix products, contract_last(): lax.dot_general(left_side, right_side, (((1,), (1,)), ((), ())), preferre...  27.3 us
    dot_general x41, matrix products, contract_first(): lax.dot_general(left_side, right_side, (((0,), (0,)), ((), ())), preferre...  18.4 us
    all_gather x1, blocking collectives, local(): lax.all_gather(grad_dot, 'ctx', axis=0, tiled=True)  14.1 us
    all_gather x1, blocking collectives, local(): lax.all_gather(log_norm, 'ctx', axis=0, tiled=True)  14.1 us
  transfers between devices with their start and end apart: 9, of which 6 were waited for; matrix products, arithmetic and copies ran while one was open for 26% of the time, Pallas kernels for 0%

profile of v1, /device:TPU:0, one launch (start us, length us, event | category | flops | bytes accessed | tf_op | source)
XLA Modules:
  0.0 468.5 jit_solution(12447787833063976131)
XLA Ops:
  9.7 36.5 %all-gather.10.cloned.1.call-done = bf16[1,1024,1280]{2,1,0:T(8,128)(2,1)} async-done(((bf16[1,128,1280]{2,1,0:T(8,128)(2,1)}), bf16[1,1024,1280]{2,1,0:T(8,128)(2,1)}) %all-gather.10.cloned.1.call-update) | async-done | bytes 2621456 | tf_op jit(solution)/shard_map/all_gather | solution.py:207
  46.3 34.5 %all-gather.12.cloned.1.call-done = bf16[1,1024,1280]{2,1,0:T(8,128)(2,1)} async-done(((bf16[1,128,1280]{2,1,0:T(8,128)(2,1)}), bf16[1,1024,1280]{2,1,0:T(8,128)(2,1)}) %all-gather.12.cloned.1.call-update) | async-done | bytes 2621456 | tf_op jit(solution)/shard_map/all_gather | solution.py:208
  80.8 48.6 %while.152 = (s32[]{:T(128)}, bf16[128,1280]{1,0:T(8,128)(2,1)S(1)}, f32[128,10]{0,1:T(8,128)S(1)}, f32[10,128,1024]{2,1,0:T(8,128)}, bf16[128,1280]{1,0:T(8,128...) while((s32[]{:T(128)}, bf16[128,1280]{1,0:T(8,128)(2,1)S(1)}, ...), condition=%wide.region_9.10_spmd, body=%wide.region_2.9_spmd.sunk | while | flops 51233556 | bytes 3044097 | solution.py:98
  85.7 2.0 bitcast_dynamic-update-slice_fusion.2
  95.4 2.0 bitcast_dynamic-update-slice_fusion.2
  100.3 2.0 bitcast_dynamic-update-slice_fusion.2
  105.1 2.0 bitcast_dynamic-update-slice_fusion.2
  110.0 2.0 bitcast_dynamic-update-slice_fusion.2
  114.9 2.0 bitcast_dynamic-update-slice_fusion.2
  119.7 2.0 bitcast_dynamic-update-slice_fusion.2
  124.6 2.0 bitcast_dynamic-update-slice_fusion.2
  129.5 4.6 convolution_convert_fusion
  135.6 68.3 %collective-permute-done = bf16[320,2560]{1,0:T(8,128)(2,1)S(1)} collective-permute-done((bf16[320,2560]{1,0:T(8,128)(2,1)S(1)}, bf16[320,2560]{1,0:T(8,128)(2,1)S(1)}, u32[]{:S(2)}, u32[]{:S(2)}) %collective-permute-start) | collective-permute-done | bytes 1638432 | tf_op jit(solution)/shard_map/ppermute | solution.py:201
  206.8 54.1 %collective-permute-done.1 = bf16[320,2560]{1,0:T(8,128)(2,1)} collective-permute-done((bf16[320,2560]{1,0:T(8,128)(2,1)S(1)}, bf16[320,2560]{1,0:T(8,128)(2,1)}, u32[]{:S(2)}, u32[]{:S(2)}) %collective-permute-start.1) | collective-permute-done | bytes 1638432 | tf_op jit(solution)/shard_map/ppermute | solution.py:201
  261.8 36.6 %collective-permute-done.2 = bf16[320,2560]{1,0:T(8,128)(2,1)} collective-permute-done((bf16[320,2560]{1,0:T(8,128)(2,1)}, bf16[320,2560]{1,0:T(8,128)(2,1)}, u32[]{:S(2)}, u32[]{:S(2)}) %collective-permute-start.2) | collective-permute-done | bytes 1638432 | tf_op jit(solution)/shard_map/ppermute | solution.py:201
  305.1 4.7 %copy-done.4 = bf16[2560,2560]{1,0:T(8,128)(2,1)} copy-done((bf16[2560,2560]{1,0:T(8,128)(2,1)}, bf16[2560,2560]{1,0:T(8,128)(2,1)S(1)}, u32[]{:S(2)}) %copy-start.4) | copy-done | bytes 13107224
  309.8 2.7 convert_multiply_fusion
  312.5 14.1 %all_gather.22 = f32[1024,10]{0,1:T(8,128)S(1)} all-gather(f32[128,10]{0,1:T(8,128)S(1)} %get-tuple-element.2090), channel_id=1, replica_groups=mesh['dp'=4,'ctx'=8] {'ctx'}, dimensions={0}, use_global_device_ids=true | all-gather | bytes 46080 | tf_op jit(solution)/shard_map/all_gather | solution.py:221
  326.6 14.1 %all_gather.23 = f32[1024,10]{0,1:T(8,128)S(1)} all-gather(f32[128,10]{0,1:T(8,128)S(1)} %reduce_sum.32), channel_id=1, replica_groups=mesh['dp'=4,'ctx'=8] {'ctx'}, dimensions={0}, use_global_device_ids=true | all-gather | bytes 46080 | tf_op jit(solution)/shard_map/all_gather | solution.py:222
  340.8 5.9 %fusion.63 = bf16[1,128,2560]{2,1,0:T(8,128)(2,1)} fusion(bf16[128,1280]{1,0:T(8,128)(2,1)S(1)} %get-tuple-element.1124, bf16[2560,2560]{1,0:T(8,128)(2,1)} %copy-done.4, s32[]{:T(128)S(6)} %select_n.135), kind=kOutput, calls=%fused_computation.88 | convolution fusion | flops 839188480 | bytes 7536644 | tf_op jit(solution)/shard_map/dot_general | solution.py:215
  348.5 109.2 %while.155 = (s32[]{:T(128)}, bf16[128,1280]{1,0:T(8,128)(2,1)S(1)}, bf16[128,1280]{1,0:T(8,128)(2,1)S(1)}, bf16[128,1280]{1,0:T(8,128)(2,1)S(1)}, bf16[1024,128...) while((s32[]{:T(128)}, bf16[128,1280]{1,0:T(8,128)(2,1)S(1)}, ...), condition=%wide.region_16.17_spmd, body=%wide.region_11.16_spmd.sunk | while | flops 101761040 | bytes 6078972 | solution.py:185
  357.0 2.4 while.159
  367.9 2.4 while.159
  378.8 2.4 while.159
  389.8 2.4 while.159
  400.7 2.4 while.159
  411.6 2.4 while.159
  422.5 2.4 while.159
  433.4 2.4 while.159
  444.3 2.4 while.159
  455.2 2.4 while.159
  457.8 3.8 convert_element_type.87
  (655 shorter events, 179.8 us)
Async XLA Ops:
  7.2 122.3 %copy-start = (bf16[1,128,2560]{2,1,0:T(8,128)(2,1)S(1)}, bf16[1,128,2560]{2,1,0:T(8,128)(2,1)}, u32[]{:S(2)}) copy-start(bf16[1,128,2560]{2,1,0:T(8,128)(2,1)} %param.22) | copy-start | bytes 1966084
  7.2 39.1 %all-gather.10.cloned.1.call-start = ((), (), s32[]{:S(2)}) async-start(), calls=%async_computation.4 | async-start | bytes 2949120 | tf_op jit(solution)/shard_map/all_gather | solution.py:207
  7.9 72.9 %all-gather.12.cloned.1.call-start = ((), (), s32[]{:S(2)}) async-start(), calls=%async_computation.5 | async-start | bytes 2949120 | tf_op jit(solution)/shard_map/all_gather | solution.py:208
  8.7 338.0 %reduce-scatter.2.cloned.1.call-start = ((), (), s32[]{:S(2)}) async-start(), calls=%async_computation.2 | async-start | bytes 8192000 | tf_op jit(solution)/shard_map/reduce_scatter | solution.py:243
  129.5 4.7 copy-start.1
  134.1 212.6 %all-gather.14.cloned.1.call-start = ((), (), s32[]{:S(2)}) async-start(), calls=%async_computation.6 | async-start | bytes 2949120 | tf_op jit(solution)/shard_map/all_gather | solution.py:209
  134.1 69.8 %collective-permute-start = (bf16[320,2560]{1,0:T(8,128)(2,1)S(1)}, bf16[320,2560]{1,0:T(8,128)(2,1)S(1)}, u32[]{:S(2)}, u32[]{:S(2)}) collective-permute-start(bf16[320,2560]{1,0:T(8,128)(2,1)S(1)} %copy-done.1), channel_id=1, source_target_pairs={{0,8},{8,16},{16,24},{24,0},{1,9},{9,17},{17,25},{25,1},{2,10},{10... | collective-permute-start | bytes 4915208 | tf_op jit(solution)/shard_map/ppermute | solution.py:201
  203.9 1.2 copy-start.2
  205.1 55.8 %collective-permute-start.1 = (bf16[320,2560]{1,0:T(8,128)(2,1)S(1)}, bf16[320,2560]{1,0:T(8,128)(2,1)}, u32[]{:S(2)}, u32[]{:S(2)}) collective-permute-start(bf16[320,2560]{1,0:T(8,128)(2,1)S(1)} %collective-permute-done), channel_id=1, source_target_pairs={{0,8},{8,16},{16,24},{24,0},{1,9},{9,17},{17,25},{25,1},{2,10},{10... | collective-permute-start | bytes 4915208 | tf_op jit(solution)/shard_map/ppermute | solution.py:201
  260.9 37.5 %collective-permute-start.2 = (bf16[320,2560]{1,0:T(8,128)(2,1)}, bf16[320,2560]{1,0:T(8,128)(2,1)}, u32[]{:S(2)}, u32[]{:S(2)}) collective-permute-start(bf16[320,2560]{1,0:T(8,128)(2,1)} %collective-permute-done.1), channel_id=1, source_target_pairs={{0,8},{8,16},{16,24},{24,0},{1,9},{9,17},{17,25},{25,1},{2,10},{10... | collective-permute-start | bytes 4915208 | tf_op jit(solution)/shard_map/ppermute | solution.py:201
  261.5 86.9 %all-gather.8.cloned.1.call-start = ((), (), s32[]{:S(2)}) async-start(), calls=%async_computation.1 | async-start | bytes 2949120 | tf_op jit(solution)/shard_map/all_gather | solution.py:210
  261.8 39.7 %copy-start.3 = (bf16[320,2560]{1,0:T(8,128)(2,1)S(1)}, bf16[320,2560]{1,0:T(8,128)(2,1)}, u32[]{:S(2)}) copy-start(bf16[320,2560]{1,0:T(8,128)(2,1)} %copy-done.2) | copy-start | bytes 4915204
  305.1 4.7 %copy-start.4 = (bf16[2560,2560]{1,0:T(8,128)(2,1)}, bf16[2560,2560]{1,0:T(8,128)(2,1)S(1)}, u32[]{:S(2)}) copy-start(bf16[2560,2560]{1,0:T(8,128)(2,1)S(1)} %constant_dynamic-update-slice_fusion) | copy-start | bytes 39321604
  312.5 145.3 %all-reduce.2.cloned.1.call-start = ((), (), s32[]{:S(2)}) async-start(), calls=%async_computation.3 | async-start | bytes 3276800 | tf_op jit(solution)/shard_map/psum | solution.py:249
  457.7 3.9 copy-start.5
  457.7 3.9 copy-start.6
  457.7 3.9 copy-start.7
Sparse Core Ops, SparseCore 0:
  9.7 36.5 all-gather.9
  47.9 32.8 all-gather.11
  134.2 121.3 reduce-scatter.1
  261.6 32.8 all-gather.13
  312.6 35.7 all-gather.7
  350.7 60.7 all-reduce.1
